TPU v7x, 32 devices: a whole 2x2x4 slice. The times are simulated.
32 devices in a mesh: age: 8 (over y, x, core), box: 4 (over z).
Axes of the slice: x: 2, y: 2, z: 4, core: 2. Of those that a mesh axis runs over, the one named last changes fastest.
Arguments:
- position: float32 [3, 131072], P(None, ('age', 'box')), may hold values from -6 to 6
- strength: float32 [3, 131072], P(None, ('age', 'box')), may hold values from -6 to 6
- node_box: int32 [131072], P(('age', 'box')), may hold values from 0 to 1023, as said below
- box_order: int32 [1024], P(('age', 'box')), may hold values from 0 to 1023, as said below
- box_center: float32 [3, 1024], P(None, ('age', 'box')), may hold values from -6 to 6
- near_list: int32 [1024, 4], P(('age', 'box')), may hold values from -1 to 1023, as said below
- m2l_source: int32 [1024, 32], P(('age', 'box')), may hold values from 0 to 1023
- m2l_type: int32 [1024, 32], P(('age', 'box')), may hold values from 0 to 15
- basis_dir: float32 [3, 256], replicated, may hold values from -3.5 to 3.5
- basis_freq: float32 [3, 256], replicated, may hold values from -6 to 6
- basis_phase: float32 [256], replicated, may hold values from -3.140625 to 3.140625
- translation: bfloat16 [16, 256, 256], replicated, may hold values from -0.0012207031 to 0.0012207031
Outputs:
- velocity: float32 [3, 131072], P(None, ('age', 'box'))
Inputs may be any that keep to these rules, and one draw needn't show every extreme that they name: box_order is a permutation of the box ids. `node_box`: every entry is a box id. Of the 4096 nodes of one device (aligned blocks of 4096 entries), at most 256 lie in the boxes held by any one device, that is the boxes box_order[g * 32] to box_order[g * 32 + 31]; in every draw some device holds the boxes of exactly 256 nodes of every device. Over all nodes, at most 256 lie in any one box, and in every draw some box holds exactly 256. `near_list`: row p lists box_order[p] first, then distinct other boxes held by the same device as position p, then -1 padding. `m2l_source`: entries are box ids; repeats may occur.
All inputs are finite; a program needn't handle non-finite values.
Results may differ from a plain program's by a relative error of at most 0.0025.
Values may be sent and summed in bfloat16 or wider, within the bound.
A program may use at most 64 MiB of HBM per device.

v0:
```python
import functools

import jax
import jax.numpy as jnp
import numpy as np
from jax import lax
from jax.experimental import pallas as pl
from jax.experimental.pallas import tpu as pltpu
from jax.sharding import PartitionSpec as P

AXES = ("age", "box")
core_square = 0.01
inv_four_pi = 0.07957747154594767
inv_two_pi = 0.15915494309189535
LANES = 128
VMEM_LIMIT = 32 * 1024 * 1024
SMALL_LIMIT = 6 * 1024 * 1024


def cos_coefficients(degree):
    nodes = np.cos(np.pi * (np.arange(64) + 0.5) / 64)
    w = 0.125 * (nodes + 1.0)
    fit = np.polynomial.chebyshev.Chebyshev.fit(
        w, np.cos(2 * np.pi * np.sqrt(w)), degree, domain=[0, 0.25]
    )
    return [float(c) for c in fit.convert(kind=np.polynomial.Polynomial).coef]


COS_COEF = cos_coefficients(6)


def cos_turns(turns):
    v = turns - ((turns + 12582912.0) - 12582912.0)
    w = v * v
    acc = jnp.full_like(w, COS_COEF[-1])
    for c in COS_COEF[-2::-1]:
        acc = acc * w + c
    return acc


def gather_body(n_age, n_box, x_ref, o_ref, send_sem, recv_sem):
    me_age, me_box = lax.axis_index("age"), lax.axis_index("box")
    barrier = pltpu.get_barrier_semaphore()

    def on_box(d):
        return {"age": me_age, "box": lax.rem(me_box + d, n_box)}

    def on_age(d):
        return {"age": lax.rem(me_age + d, n_age), "box": me_box}

    def greet(peer):
        def step(d, carry):
            pl.semaphore_signal(
                barrier, inc=1, device_id=peer(d), device_id_type=pl.DeviceIdType.MESH
            )
            return carry

        return step

    lax.fori_loop(1, n_box, greet(on_box), 0)
    lax.fori_loop(1, n_age, greet(on_age), 0)
    o_ref[me_age, me_box] = x_ref[...]
    pl.semaphore_wait(barrier, n_box - 1 + n_age - 1)

    def along_box(d):
        return pltpu.make_async_remote_copy(
            src_ref=x_ref,
            dst_ref=o_ref.at[me_age, me_box],
            send_sem=send_sem.at[d - 1],
            recv_sem=recv_sem.at[d - 1],
            device_id=on_box(d),
            device_id_type=pl.DeviceIdType.MESH,
        )

    def along_age(d):
        return pltpu.make_async_remote_copy(
            src_ref=o_ref.at[me_age],
            dst_ref=o_ref.at[me_age],
            send_sem=send_sem.at[n_box - 2 + d],
            recv_sem=recv_sem.at[n_box - 2 + d],
            device_id=on_age(d),
            device_id_type=pl.DeviceIdType.MESH,
        )

    def start(copy):
        def step(d, carry):
            copy(d).start()
            return carry

        return step

    def finish(copy):
        def step(d, carry):
            copy(d).wait()
            return carry

        return step

    lax.fori_loop(1, n_box, start(along_box), 0)
    lax.fori_loop(1, n_box, finish(along_box), 0)
    lax.fori_loop(1, n_age, start(along_age), 0)
    lax.fori_loop(1, n_age, finish(along_age), 0)


def gather_blocks(x, n_age, n_box, collective_id):
    copies = n_age + n_box - 2
    return pl.pallas_call(
        functools.partial(gather_body, n_age, n_box),
        out_shape=jax.ShapeDtypeStruct((n_age, n_box) + x.shape, x.dtype),
        in_specs=[pl.BlockSpec(memory_space=pltpu.VMEM)],
        out_specs=pl.BlockSpec(memory_space=pltpu.VMEM),
        scratch_shapes=[
            pltpu.SemaphoreType.DMA((copies,)),
            pltpu.SemaphoreType.DMA((copies,)),
        ],
        compiler_params=pltpu.CompilerParams(
            collective_id=collective_id, has_side_effects=True, vmem_limit_bytes=SMALL_LIMIT
        ),
    )(x)


def exchange_body(n_box, n, x_ref, o_ref, send_sem, recv_sem):
    me = lax.axis_index("age") * n_box + lax.axis_index("box")
    barrier = pltpu.get_barrier_semaphore()

    def place(other):
        return {"age": other // n_box, "box": lax.rem(other, n_box)}

    def greet(d, carry):
        pl.semaphore_signal(
            barrier,
            inc=1,
            device_id=place(lax.rem(me + d, n)),
            device_id_type=pl.DeviceIdType.MESH,
        )
        return carry

    lax.fori_loop(1, n, greet, 0)
    o_ref[me] = x_ref[me]
    pl.semaphore_wait(barrier, n - 1)

    def copy(d):
        other = lax.rem(me + d, n)
        return pltpu.make_async_remote_copy(
            src_ref=x_ref.at[other],
            dst_ref=o_ref.at[me],
            send_sem=send_sem.at[d - 1],
            recv_sem=recv_sem.at[d - 1],
            device_id=place(other),
            device_id_type=pl.DeviceIdType.MESH,
        )

    def send(d, carry):
        copy(d).start()
        return carry

    def finish(d, carry):
        copy(d).wait()
        return carry

    lax.fori_loop(1, n, send, 0)
    lax.fori_loop(1, n, finish, 0)


def exchange(x, n_box, collective_id):
    n = x.shape[0]
    return pl.pallas_call(
        functools.partial(exchange_body, n_box, n),
        out_shape=jax.ShapeDtypeStruct(x.shape, x.dtype),
        in_specs=[pl.BlockSpec(memory_space=pltpu.VMEM)],
        out_specs=pl.BlockSpec(memory_space=pltpu.VMEM),
        scratch_shapes=[
            pltpu.SemaphoreType.DMA((n - 1,)),
            pltpu.SemaphoreType.DMA((n - 1,)),
        ],
        compiler_params=pltpu.CompilerParams(
            collective_id=collective_id, has_side_effects=True, vmem_limit_bytes=SMALL_LIMIT
        ),
    )(x)


def load_lanes(ref, i):
    if len(ref.shape) == 2:
        return ref[:, pl.ds(pl.multiple_of(i * LANES, LANES), LANES)]
    per = ref.shape[2]
    if per >= LANES:
        k = per // LANES
        return ref[i // k, :, pl.ds(pl.multiple_of(lax.rem(i, k) * LANES, LANES), LANES)]
    m = LANES // per
    return jnp.concatenate([ref[i * m + u] for u in range(m)], axis=1)


def store_lanes(ref, i, tile):
    if len(ref.shape) == 2:
        ref[:, pl.ds(pl.multiple_of(i * LANES, LANES), LANES)] = tile
        return
    per = ref.shape[2]
    if per >= LANES:
        k = per // LANES
        ref[i // k, :, pl.ds(pl.multiple_of(lax.rem(i, k) * LANES, LANES), LANES)] = tile
        return
    m = LANES // per
    for u in range(m):
        ref[i * m + u] = tile[:, u * per : (u + 1) * per]


def columns(ref):
    return ref.shape[-1] if len(ref.shape) == 2 else ref.shape[0] * ref.shape[2]


def lanes_to_rows(tile):
    padded = jnp.concatenate([tile, jnp.zeros((LANES - tile.shape[0], LANES), tile.dtype)], axis=0)
    return padded.T


def fill_rows(src_ref, rows_ref, count):
    def step(i, carry):
        at = pl.multiple_of(i * LANES, LANES)
        rows_ref[pl.ds(at, LANES), :] = lanes_to_rows(load_lanes(src_ref, i))
        return carry

    lax.fori_loop(0, count // LANES, step, 0, unroll=8)


def take_lanes(rows_ref, out_ref, count):
    def step(i, carry):
        at = pl.multiple_of(i * LANES, LANES)
        store_lanes(out_ref, i, rows_ref[pl.ds(at, LANES), :].T[:8])
        return carry

    lax.fori_loop(0, count // LANES, step, 0, unroll=8)


def zero_rows(ref):
    def step(i, carry):
        at = pl.multiple_of(i * 8, 8)
        ref[pl.ds(at, 8), :] = jnp.zeros((8, LANES), jnp.float32)
        return carry

    lax.fori_loop(0, ref.shape[0] // 8, step, 0, unroll=8)


def scatter_rows(idx_ref, src_ref, dst_ref, count):
    def step(i, carry):
        at = pl.multiple_of(i * 16, 16)
        block = src_ref[pl.ds(at, 16), :]
        for u in range(16):
            dst_ref[pl.ds(idx_ref[at + u], 1), :] = block[u : u + 1, :]
        return carry

    lax.fori_loop(0, count // 16, step, 0)


def gather_rows(idx_ref, src_ref, dst_ref, count):
    def step(i, carry):
        at = pl.multiple_of(i * 16, 16)
        rows = [src_ref[pl.ds(idx_ref[at + u], 1), :] for u in range(16)]
        dst_ref[pl.ds(at, 16), :] = jnp.concatenate(rows, axis=0)
        return carry

    lax.fori_loop(0, count // 16, step, 0)


def spread_body(idx_ref, x_ref, out_ref, rows, placed):
    fill_rows(x_ref, rows, columns(x_ref))
    zero_rows(placed)
    scatter_rows(idx_ref, rows, placed, columns(x_ref))
    take_lanes(placed, out_ref, columns(out_ref))


def collect_body(idx_ref, x_ref, out_ref, src, rows):
    fill_rows(x_ref, src, columns(x_ref))
    gather_rows(idx_ref, src, rows, columns(out_ref))
    take_lanes(rows, out_ref, columns(out_ref))


def permute_call(body, idx, x, out_shape, scratch_rows):
    return pl.pallas_call(
        body,
        out_shape=jax.ShapeDtypeStruct(out_shape, jnp.float32),
        in_specs=[
            pl.BlockSpec(memory_space=pltpu.SMEM),
            pl.BlockSpec(memory_space=pltpu.VMEM),
        ],
        out_specs=pl.BlockSpec(memory_space=pltpu.VMEM),
        scratch_shapes=[pltpu.VMEM((r, LANES), jnp.float32) for r in scratch_rows],
        compiler_params=pltpu.CompilerParams(vmem_limit_bytes=VMEM_LIMIT),
    )(idx, x)


def ranks(key, kinds):
    count = key.shape[0]
    blocks = count // LANES
    hits = (key[None, :] == jnp.arange(kinds, dtype=jnp.int32)[:, None]).reshape(
        kinds, blocks, LANES
    )
    hits16 = hits.astype(jnp.bfloat16)
    lane = np.arange(LANES)
    before = jnp.asarray(lane[:, None] < lane[None, :], jnp.bfloat16)
    inside = jnp.dot(
        hits16.reshape(kinds * blocks, LANES), before, preferred_element_type=jnp.float32
    ).reshape(kinds, blocks, LANES)
    totals = jnp.sum(hits.astype(jnp.float32), axis=2)
    block = np.arange(blocks)
    base = jnp.dot(
        totals.astype(jnp.bfloat16),
        jnp.asarray(block[:, None] < block[None, :], jnp.bfloat16),
        preferred_element_type=jnp.float32,
    )
    rank = jnp.sum(jnp.where(hits, inside + base[:, :, None], 0.0), axis=0)
    return rank.reshape(count).astype(jnp.int32)


def split16(x, parts):
    pieces = []
    for _ in range(parts):
        piece = x.astype(jnp.bfloat16).astype(jnp.float32)
        pieces.append(piece)
        x = x - piece
    return pieces


def stack16(x, parts):
    pieces = split16(x, parts)
    rows = x.shape[0] * parts
    if rows % 16:
        pieces.append(jnp.zeros((16 - rows % 16, x.shape[1]), jnp.float32))
    return jnp.concatenate(pieces, axis=0).astype(jnp.bfloat16)


def cross_parts(a, b):
    return (
        a[1:2] * b[2:3] - a[2:3] * b[1:2],
        a[2:3] * b[0:1] - a[0:1] * b[2:3],
        a[0:1] * b[1:2] - a[1:2] * b[0:1],
    )


def one_box(b, center_ref, basis_ref, freq_ref, rows_ref, block_ref, wave_ref, lanes_ref, parts_ref):
    count = lanes_ref.shape[2]
    at = pl.multiple_of(b * count, count)
    coef = basis_ref.shape[1]
    cx, cy, cz = center_ref[0, b], center_ref[1, b], center_ref[2, b]
    lanes = jnp.concatenate(
        [rows_ref[pl.ds(at + i * LANES, LANES), :].T[:8] for i in range(count // LANES)], axis=1
    )
    lanes_ref[b] = lanes
    zero = jnp.zeros((1, count), jnp.float32)
    table = jnp.concatenate(
        [lanes[3:6], zero, *cross_parts(lanes[3:6], lanes[0:3]), zero], axis=0
    )
    parts = stack16(table, 3)
    parts_ref[b] = parts
    one = jnp.ones((1, count), jnp.float32)
    offset = jnp.concatenate(
        [lanes[0:1] - cx, lanes[1:2] - cy, lanes[2:3] - cz, one, jnp.zeros((4, count), jnp.float32)],
        axis=0,
    )
    o1, o2, o3 = split16(offset, 3)
    stacked = jnp.concatenate([o3, o2, o2, o1, o1, o1], axis=0).astype(jnp.bfloat16)
    turns = lax.dot_general(
        stacked, freq_ref[...], (((0,), (0,)), ((), ())), preferred_element_type=jnp.float32
    )
    chunk = 32
    highs, lows = [], []
    for c in range(count // chunk):
        wave = cos_turns(turns[c * chunk : (c + 1) * chunk])
        high = wave.astype(jnp.bfloat16)
        highs.append(high)
        lows.append((wave - high.astype(jnp.float32)).astype(jnp.bfloat16))
    high = jnp.concatenate(highs, axis=0)
    low = jnp.concatenate(lows, axis=0)
    wave_ref[pl.ds(at, count), :coef] = high
    wave_ref[pl.ds(at, count), coef:] = low
    sums = jnp.dot(parts, high, preferred_element_type=jnp.float32)
    sums = sums + jnp.dot(parts, low, preferred_element_type=jnp.float32)
    sums = sums[0:8] + sums[8:16] + sums[16:24]
    block_ref[b] = (
        basis_ref[0:1, :] * sums[0:1]
        + basis_ref[1:2, :] * sums[1:2]
        + basis_ref[2:3, :] * sums[2:3]
    )


def group_body(
    idx_ref, center_ref, x_ref, basis_ref, freq_ref,
    rows_ref, block_ref, wave_ref, lanes_ref, parts_ref, scattered,
):
    fill_rows(x_ref, scattered, columns(x_ref))
    zero_rows(rows_ref)
    scatter_rows(idx_ref, scattered, rows_ref, columns(x_ref))

    def step(b, carry):
        one_box(
            b, center_ref, basis_ref, freq_ref, rows_ref, block_ref, wave_ref, lanes_ref, parts_ref
        )
        return carry

    lax.fori_loop(0, block_ref.shape[0], step, 0, unroll=2)


def split_body(x_ref, out_ref):
    f1, f2, f3 = split16(x_ref[...], 3)
    out_ref[...] = jnp.concatenate([f1, f2, f1, f3, f2, f1], axis=0).astype(jnp.bfloat16)


def split_call(x):
    return pl.pallas_call(
        split_body, out_shape=jax.ShapeDtypeStruct((6 * x.shape[0], x.shape[1]), jnp.bfloat16)
    )(x)


def group_call(idx, center, got, basis, freq, boxes, per_box):
    coef = basis.shape[1]
    slots = boxes * per_box
    return pl.pallas_call(
        group_body,
        out_shape=(
            jax.ShapeDtypeStruct((slots + 8, LANES), jnp.float32),
            jax.ShapeDtypeStruct((boxes, 1, coef), jnp.float32),
            jax.ShapeDtypeStruct((slots, 2 * coef), jnp.bfloat16),
            jax.ShapeDtypeStruct((boxes, 8, per_box), jnp.float32),
            jax.ShapeDtypeStruct((boxes, 32, per_box), jnp.bfloat16),
        ),
        in_specs=[pl.BlockSpec(memory_space=pltpu.SMEM)] * 2
        + [pl.BlockSpec(memory_space=pltpu.VMEM)] * 3,
        out_specs=(pl.BlockSpec(memory_space=pltpu.VMEM),) * 5,
        scratch_shapes=[pltpu.VMEM((slots, LANES), jnp.float32)],
        compiler_params=pltpu.CompilerParams(vmem_limit_bytes=VMEM_LIMIT),
    )(idx, center, got, basis, freq)


def one_velocity(b, near_ref, rows_ref, lanes_ref, parts_ref, wave_ref, exp_ref, dir_ref, out_ref):
    per_box = lanes_ref.shape[2]
    here = pl.multiple_of(b * per_box, per_box)
    coef = dir_ref.shape[1]
    near_count = near_ref.shape[1]
    chunk = 32

    def pair_sums(j, target):
        tx, ty, tz = target[0:1], target[1:2], target[2:3]
        pieces = []
        for c in range(per_box // chunk):
            at = pl.multiple_of(j * per_box + c * chunk, chunk)
            s = rows_ref[pl.ds(at, chunk), :]
            dx = tx - s[:, 0:1]
            dy = ty - s[:, 1:2]
            dz = tz - s[:, 2:3]
            r = lax.rsqrt(dx * dx + dy * dy + dz * dz + core_square)
            pieces.append((r * r * r).astype(jnp.bfloat16))
        factor = jnp.concatenate(pieces, axis=0)
        return jnp.dot(parts_ref[j], factor, preferred_element_type=jnp.float32)

    def whole_box(count):
        target = lanes_ref[b]
        table = stack16(dir_ref[...] * exp_ref[b], 2)
        contract = (((1,), (1,)), ((), ()))
        far = lax.dot_general(
            table,
            wave_ref[pl.ds(here, per_box), :coef],
            contract,
            preferred_element_type=jnp.float32,
        )
        far = far + lax.dot_general(
            table,
            wave_ref[pl.ds(here, per_box), coef:],
            contract,
            preferred_element_type=jnp.float32,
        )
        far = far[0:8] + far[8:16]
        sums = pair_sums(near_ref[b, 0], target)
        for v in range(1, count):
            sums = sums + pair_sums(near_ref[b, v], target)
        sums = sums[0:8] + sums[8:16] + sums[16:24]
        near = jnp.concatenate(
            [*cross_parts(sums[0:3], target[0:3]), jnp.zeros((5, per_box), jnp.float32)], axis=0
        ) - jnp.concatenate([sums[4:7], jnp.zeros((5, per_box), jnp.float32)], axis=0)
        total = near * inv_four_pi + far
        for i in range(per_box // LANES):
            out_ref[pl.ds(here + i * LANES, LANES), :] = lanes_to_rows(
                total[:, i * LANES : (i + 1) * LANES]
            )

    held = (near_ref[b, 0] >= 0).astype(jnp.int32)
    for v in range(1, near_count):
        held = held + (near_ref[b, v] >= 0).astype(jnp.int32)
    for count in range(1, near_count + 1):
        pl.when(held == count)(functools.partial(whole_box, count))


def velocity_body(
    idx_ref, near_ref, rows_ref, lanes_ref, parts_ref, wave_ref, exp_ref, dir_ref,
    out_ref, vel, rows,
):
    def step(b, carry):
        one_velocity(
            b, near_ref, rows_ref, lanes_ref, parts_ref, wave_ref, exp_ref, dir_ref, vel
        )
        return carry

    lax.fori_loop(0, lanes_ref.shape[0], step, 0)
    gather_rows(idx_ref, vel, rows, columns(out_ref))
    take_lanes(rows, out_ref, columns(out_ref))


def velocity_call(idx, out_shape, near, rows, lanes, parts, wave, exps, basis_dir):
    slots = wave.shape[0]
    return pl.pallas_call(
        velocity_body,
        out_shape=jax.ShapeDtypeStruct(out_shape, jnp.float32),
        in_specs=[pl.BlockSpec(memory_space=pltpu.SMEM)] * 2
        + [pl.BlockSpec(memory_space=pltpu.VMEM)] * 6,
        out_specs=pl.BlockSpec(memory_space=pltpu.VMEM),
        scratch_shapes=[pltpu.VMEM((slots, LANES), jnp.float32)] * 2,
        compiler_params=pltpu.CompilerParams(vmem_limit_bytes=VMEM_LIMIT),
    )(idx, near, rows, lanes, parts, wave, exps, basis_dir)


def per_device(
    n_age,
    n_box,
    position,
    strength,
    node_box,
    box_order,
    box_center,
    near_list,
    m2l_source,
    m2l_type,
    basis_dir,
    basis_freq,
    basis_phase,
    translation,
):
    groups = n_age * n_box
    node_count = position.shape[1]
    box_local = box_order.shape[0]
    slots_total = 2 * node_count
    per_peer = slots_total // groups
    per_box = slots_total // box_local
    coef = basis_phase.shape[0]
    kind_count = translation.shape[0]
    box_total = groups * box_local

    padded_order = jnp.pad(box_order, (0, LANES - box_local)).reshape(1, LANES)
    all_order = gather_blocks(padded_order, n_age, n_box, 0)[:, :, 0, :box_local].reshape(-1)

    node_slot = jnp.sum(
        jnp.where(
            node_box[None, :] == all_order[:, None],
            jnp.arange(box_total, dtype=jnp.int32)[:, None],
            0,
        ),
        axis=0,
    )
    owner = node_slot // box_local
    label = (node_slot - owner * box_local + 1).astype(jnp.float32)
    send_at = owner * per_peer + ranks(owner, groups)
    fields = jnp.concatenate(
        [position, strength, label[None, :], jnp.zeros((1, node_count), jnp.float32)], axis=0
    )
    payload = permute_call(
        spread_body, send_at, fields, (groups, 8, per_peer), (node_count, slots_total)
    )
    got = exchange(payload, n_box, 2)

    hit_source = (m2l_source[:, :, None] == all_order[None, None, :]).astype(jnp.bfloat16)
    kind_hits = (
        m2l_type[:, :, None] == jnp.arange(kind_count, dtype=jnp.int32)[None, None, :]
    ).astype(jnp.bfloat16)
    list_counts = jnp.einsum(
        "jlt,jlb->tjb", kind_hits, hit_source, preferred_element_type=jnp.float32
    )
    list_counts = list_counts.astype(jnp.bfloat16).reshape(kind_count * box_local, box_total)
    near_local = jnp.sum(
        jnp.where(
            near_list[:, :, None] == box_order[None, None, :],
            jnp.arange(1, box_local + 1, dtype=jnp.int32)[None, None, :],
            0,
        ),
        axis=2,
    ) - 1

    got_label = got[:, 6, :].reshape(-1).astype(jnp.int32) - 1
    live = got_label >= 0
    tile_at = jnp.where(
        live, got_label * per_box + ranks(got_label, box_local), slots_total
    )
    dir_rows = jnp.pad(basis_dir, ((0, 5), (0, 0)))
    waves = jnp.concatenate([basis_freq, basis_phase[None, :]], axis=0) * inv_two_pi
    freq = split_call(jnp.pad(waves, ((0, 4), (0, 0))))
    rows, sums, wave, lanes, parts = group_call(
        tile_at, box_center, got, dir_rows, freq, box_local, per_box
    )
    local_blocks = sums.reshape(box_local, coef).astype(jnp.bfloat16)
    all_blocks = gather_blocks(local_blocks, n_age, n_box, 1).reshape(box_total, coef)
    mixed = jnp.dot(list_counts, all_blocks, preferred_element_type=jnp.float32)
    mixed = mixed.astype(jnp.bfloat16).reshape(kind_count, box_local, coef)
    expansions = jnp.einsum(
        "tjc,tkc->jk", mixed, translation, preferred_element_type=jnp.float32
    )
    back = velocity_call(
        jnp.minimum(tile_at, slots_total - 1),
        (groups, 8, per_peer),
        near_local,
        rows,
        lanes,
        parts,
        wave,
        expansions.reshape(box_local, 1, coef),
        dir_rows,
    )
    returned = exchange(back, n_box, 3)
    out = permute_call(
        collect_body, send_at, returned, (8, node_count), (slots_total, node_count)
    )
    return out[:3]


def solution(mesh):
    n_box = mesh.shape["box"]
    n_age = mesh.shape["age"]
    placed = (
        P(None, AXES),
        P(None, AXES),
        P(AXES),
        P(AXES),
        P(None, AXES),
        P(AXES, None),
        P(AXES, None),
        P(AXES, None),
        P(),
        P(),
        P(),
        P(),
    )
    return jax.shard_map(
        functools.partial(per_device, n_age, n_box),
        mesh=mesh,
        in_specs=placed,
        out_specs=P(None, AXES),
        check_vma=False,
    )
```

profile of v0, /device:TPU:0, one launch (start us, length us, event | category | flops | bytes accessed | tf_op | source)
XLA Modules:
  0.0 142.5 jit_solution(14910717898718062985)
XLA Ops:
  0.0 0.0 copy-start
  0.0 0.0 copy-start.4
  0.0 0.0 copy-start.3
  0.0 0.8 pad_bitcast_fusion.x_ref
  0.8 0.1 pad.20.clone
  0.9 0.9 select_reduce_fusion.1
  1.8 0.7 maximum_multiply_fusion
  2.5 0.6 pad.14.x_ref
  3.1 0.7 pad.13.basis_ref.dir_ref
  3.8 0.1 copy.25
  3.9 11.4 %shard_map.154 = s32[8,4,1,128]{3,2,1,0:T(1,128)S(1)} custom-call(s32[1,128]{1,0:T(1,128)S(1)} %pad_bitcast_fusion.x_ref), custom_call_target="tpu_custom_call" | custom-call | tf_op jit(solution)/shard_map/pallas_call | solution.py:107
  15.4 0.1 slice_reduce_fusion
  15.4 0.1 eq.87
  15.5 3.0 %select_reduce_fusion = s32[4096]{0:T(1024)S(1)} fusion(s32[4096]{0:T(1024)} %param.18, s32[1024]{0:T(1024)S(1)} %eq.87), kind=kLoop, calls=%fused_computation | loop fusion | flops 12578816 | bytes 36864 | tf_op jit(solution)/shard_map/reduce_sum | solution.py:548
  18.6 0.2 convert_reduce_fusion.1
  18.8 0.8 fusion.32
  19.6 0.0 copy-start.2
  19.6 1.0 fusion.13
  20.7 0.1 add_convert_fusion
  20.8 1.3 shard_map.157.freq_ref
  22.1 0.0 copy-start.1
  22.1 1.0 maximum_maximum_fusion.x_ref
  23.0 8.2 %shard_map.155.x_ref = f32[32,8,256]{2,1,0:T(8,128)S(1)} custom-call(s32[4096]{0:T(1024)S(1)} %fusion.20.idx_ref, f32[8,4096]{1,0:T(8,128)S(1)} %maximum_maximum_fusion.x_ref), custom_call_target="tpu_custom_call" | custom-call | tf_op jit(solution)/shard_map/pallas_call | solution.py:278
  31.2 12.1 %shard_map.156.x_ref = f32[32,8,256]{2,1,0:T(8,128)S(1)} custom-call(f32[32,8,256]{2,1,0:T(8,128)S(1)} %shard_map.155.x_ref), custom_call_target="tpu_custom_call" | custom-call | tf_op jit(solution)/shard_map/pallas_call | solution.py:167
  43.3 0.1 broadcast_multiply_fusion
  43.3 0.4 convert_reduce_fusion
  43.7 0.8 fusion.31
  44.5 0.1 compare_reduce_fusion
  44.6 1.1 fusion.11
  45.8 0.0 copy-done.4
  45.8 0.0 copy-done.3
  45.8 0.9 fusion.7
  46.7 0.6 copy.27
  47.3 0.0 copy-done.2
  47.3 0.0 copy-done.1
  47.3 24.9 %shard_map.158 = (f32[8200,128]{1,0:T(8,128)S(1)}, f32[32,1,256]{2,1,0:T(1,128)S(1)}, bf16[8192,512]{1,0:T(8,128)(2,1)S(1)}, f32[32,8,256]{2,1,0:T(8,128)S(1)}, bf16[32,32,256]{2,1,0:T(8,128)(2,1)S(1)}) custom-call(s32[8192]{0:T(1024)S(1)} %get-tuple-element.16.idx_ref, f32[3,32]{1,0:T(4,128)S(1)} %copy-done.2, f32[32,8,256]{2,1,0:T(8,128)S(1)} %shard_map.156.x_ref, ...), custom_call_target="tpu_custom_call" | custom-call | tf_op jit(solution)/shard_map/pallas_call | solution.py:416
  72.2 12.5 %shard_map.159 = bf16[8,4,32,256]{3,2,1,0:T(8,128)(2,1)S(1)} custom-call(bf16[32,256]{1,0:T(8,128)(2,1)S(1)} %bitcast.52), custom_call_target="tpu_custom_call" | custom-call | tf_op jit(solution)/shard_map/pallas_call | solution.py:107
  84.8 0.4 convolution_convert_fusion
  85.2 0.0 copy-done
  85.2 0.7 convolution_bitcast_fusion
  86.0 35.1 %shard_map.160.x_ref = f32[32,8,256]{2,1,0:T(8,128)S(1)} custom-call(s32[8192]{0:T(1024)S(1)} %get-tuple-element.15.idx_ref, s32[32,4]{1,0:T(8,128)S(1)} %broadcast_add_fusion.near_ref, f32[8200,128]{1,0:T(8,128)S(1)} %get-tuple-element.10.rows_ref, f32[32,8,256]{2,1,0:T(8,128)S(1)} %get-tuple-element.11.lanes_ref, ...), custom_call_target="tpu_custom_call" | custom-call | tf_op jit(solution)/shard_map/pallas_call | solution.py:508
  121.1 12.8 %shard_map.161.x_ref = f32[32,8,256]{2,1,0:T(8,128)S(1)} custom-call(f32[32,8,256]{2,1,0:T(8,128)S(1)} %shard_map.160.x_ref), custom_call_target="tpu_custom_call" | custom-call | tf_op jit(solution)/shard_map/pallas_call | solution.py:167
  133.9 7.9 %shard_map.162 = f32[8,4096]{1,0:T(8,128)S(1)} custom-call(s32[4096]{0:T(1024)S(1)} %fusion.20.idx_ref, f32[32,8,256]{2,1,0:T(8,128)S(1)} %shard_map.161.x_ref), custom_call_target="tpu_custom_call" | custom-call | tf_op jit(solution)/shard_map/pallas_call | solution.py:278
  141.8 0.6 slice.12
  (8 shorter events, 0.1 us)
Async XLA Ops:
  0.0 85.2 %copy-start = (bf16[16,256,256]{2,1,0:T(8,128)(2,1)S(1)}, bf16[16,256,256]{2,1,0:T(8,128)(2,1)}, u32[]{:S(2)}) copy-start(bf16[16,256,256]{2,1,0:T(8,128)(2,1)} %param.27) | copy-start | bytes 6291460
  0.0 45.8 %copy-start.4 = (s32[32,32]{1,0:T(8,128)S(1)}, s32[32,32]{1,0:T(8,128)}, u32[]{:S(2)}) copy-start(s32[32,32]{1,0:T(8,128)} %param.23) | copy-start | bytes 12292
  0.0 45.8 %copy-start.3 = (s32[32,32]{1,0:T(8,128)S(1)}, s32[32,32]{1,0:T(8,128)}, u32[]{:S(2)}) copy-start(s32[32,32]{1,0:T(8,128)} %param.22) | copy-start | bytes 12292
  19.6 27.7 %copy-start.2 = (f32[3,32]{1,0:T(4,128)S(1)}, f32[3,32]{1,0:T(4,128)}, u32[]{:S(2)}) copy-start(f32[3,32]{1,0:T(4,128)} %center_ref.1) | copy-start | bytes 1156
  22.1 25.2 %copy-start.1 = (bf16[48,256]{1,0:T(8,128)(2,1)S(1)}, bf16[48,256]{1,0:T(8,128)(2,1)}, u32[]{:S(2)}) copy-start(bf16[48,256]{1,0:T(8,128)(2,1)} %shard_map.157.freq_ref) | copy-start | bytes 73732
where the time goes:
time: 143 us; the launch traced here: 142 us
  Pallas kernels  126 us (88%)
  other arithmetic  6.5 us (5%)
  matrix products  5.79 us (4%)
  local copies, waits for them, and re-layouts  3.71 us (3%)
    pallas_call x1, Pallas kernels, velocity_call(): pl.pallas_call(velocity_body, out_shape=jax.ShapeDtypeStruct(out_shape, j...  35.1 us
    pallas_call x1, Pallas kernels, group_call(): pl.pallas_call(group_body, out_shape=(jax.ShapeDtypeStruct((slots + 8, LA...  24.9 us
    pallas_call x2, Pallas kernels, exchange(): pl.pallas_call(functools.partial(exchange_body, n_box, n), out_shape=jax....  24.9 us
    pallas_call x2, Pallas kernels, gather_blocks(): pl.pallas_call(functools.partial(gather_body, n_age, n_box), out_shape=ja...  24 us
    pallas_call x2, Pallas kernels, permute_call(): pl.pallas_call(body, out_shape=jax.ShapeDtypeStruct(out_shape, jnp.float3...  16.1 us
    reduce_sum x1, other arithmetic, per_device(): jnp.sum(jnp.where(node_box[None, :] == all_order[:, None], jnp.arange(box...  3.03 us

commit v1 on v0

v1 whole, which is shorter than its diff:
```python
import functools

import jax
import jax.numpy as jnp
import numpy as np
from jax import lax
from jax.experimental import pallas as pl
from jax.experimental.pallas import tpu as pltpu
from jax.sharding import PartitionSpec as P

AXES = ("age", "box")
MESH = pl.DeviceIdType.MESH
core_square = 0.01
inv_four_pi = 0.07957747154594767
inv_two_pi = 0.15915494309189535
LANES = 128
WIDE = 256
VMEM_LIMIT = 56 * 1024 * 1024
f32, bf16, i32 = jnp.float32, jnp.bfloat16, jnp.int32
NN = (((1,), (0,)), ((), ()))
NT = (((1,), (1,)), ((), ()))


def cos_coefficients(degree):
    nodes = np.cos(np.pi * (np.arange(64) + 0.5) / 64)
    w = 0.125 * (nodes + 1.0)
    fit = np.polynomial.chebyshev.Chebyshev.fit(
        w, np.cos(2 * np.pi * np.sqrt(w)), degree, domain=[0, 0.25]
    )
    return [float(c) for c in fit.convert(kind=np.polynomial.Polynomial).coef]


COS_COEF = cos_coefficients(6)


def cos_turns(turns):
    v = turns - ((turns + 12582912.0) - 12582912.0)
    w = v * v
    acc = jnp.full_like(w, COS_COEF[-1])
    for c in COS_COEF[-2::-1]:
        acc = acc * w + c
    return acc


def dot(a, b, dims=NN):
    return lax.dot_general(a, b, dims, preferred_element_type=f32)


def sublane(rows, n):
    return lax.broadcasted_iota(i32, (rows, n), 0)


def hot(row, rows, start=0):
    steps = (sublane(rows, row.shape[1]) + start).astype(f32).astype(bf16)
    return jnp.where(row.astype(bf16) == steps, jnp.ones((), bf16), jnp.zeros((), bf16))


def pieces(x, count):
    out = []
    for _ in range(count):
        piece = x.astype(bf16).astype(f32)
        out.append(piece)
        x = x - piece
    return out


def two(x):
    return jnp.concatenate(pieces(x, 2), axis=0).astype(bf16)


def cross_parts(a, b):
    return (
        a[1:2] * b[2:3] - a[2:3] * b[1:2],
        a[2:3] * b[0:1] - a[0:1] * b[2:3],
        a[0:1] * b[1:2] - a[1:2] * b[0:1],
    )


def before_table():
    row = sublane(LANES, 2 * LANES)
    col = lax.broadcasted_iota(i32, (LANES, 2 * LANES), 1)
    return jnp.where((row < col) | (col >= LANES), 1.0, 0.0).astype(bf16)


def ranks(hits, before, carry):
    kinds = hits[0].shape[0]
    sums = dot(jnp.concatenate([h.astype(bf16) for h in hits], axis=0), before)
    out = []
    for k, h in enumerate(hits):
        part = sums[k * kinds : (k + 1) * kinds]
        out.append(jnp.sum(h * (part[:, :LANES] + carry), axis=0, keepdims=True))
        carry = carry + part[:, LANES:]
    return out, carry


class Sizes:
    def __init__(self, n_age, n_box, nodes, boxes, coef, kinds, entries, near):
        self.n_age, self.n_box, self.nodes, self.boxes = n_age, n_box, nodes, boxes
        self.coef, self.kinds, self.entries, self.near = coef, kinds, entries, near
        self.groups = n_age * n_box
        self.box_total = self.groups * boxes
        self.digits = self.box_total // 32
        self.slots = 2 * nodes
        self.per_peer = self.slots // self.groups
        self.per_box = self.slots // boxes
        self.per_chunk = WIDE // self.per_peer
        self.chunks = self.slots // WIDE
        self.batch = min(8, self.chunks)


def body(
    z,
    pos, stg, node_box, order, center, near_t, source_t, kind, direction, freq, phase, translation,
    out,
    order_own, order_all, order_row, pay, recv, blocks, back, returned,
    near_vm, near_sm, trans, fields, hot_src, owner_row, a_buf, hot_dst, label_dst,
    grouped, lanes, parts, src_tab, tgt_tab, freq_t, wave_hi, wave_lo, sums_f, counts, mixed,
    near_vel, vel, local_sem, order_sem, node_sem, block_sem, back_sem,
):
    groups, n_box, n_age = z.groups, z.n_box, z.n_age
    me_age, me_box = lax.axis_index("age"), lax.axis_index("box")
    me = me_age * n_box + me_box
    barrier = pltpu.get_barrier_semaphore()

    def place(other):
        return {"age": other // n_box, "box": lax.rem(other, n_box)}

    def ahead(d):
        return lax.rem(me + d, groups)

    def behind(d):
        return lax.rem(me + groups - d, groups)

    def loop(lo, hi, f):
        def step(i, carry):
            f(i)
            return carry

        lax.fori_loop(lo, hi, step, 0)

    loop(
        1, groups,
        lambda d: pl.semaphore_signal(
            barrier, inc=1, device_id=place(ahead(d)), device_id_type=MESH
        ),
    )
    load_translation = pltpu.make_async_copy(translation, trans, local_sem.at[0])
    load_translation.start()
    order_own[...] = jnp.full((1, LANES), -1, i32)
    order_own[:, : z.boxes] = order[...]
    order_all[me] = order_own[...]
    pl.semaphore_wait(barrier, groups - 1)

    def order_copy(d):
        return pltpu.make_async_remote_copy(
            src_ref=order_own,
            dst_ref=order_all.at[me],
            send_sem=order_sem.at[0, d - 1],
            recv_sem=order_sem.at[1, d - 1],
            device_id=place(ahead(d)),
            device_id_type=MESH,
        )

    loop(1, groups, lambda d: order_copy(d).start())

    waves = jnp.concatenate(
        [freq[...], phase[...], jnp.zeros((4, z.coef), f32)], axis=0
    ) * inv_two_pi
    f1, f2, f3 = pieces(waves, 3)
    table = jnp.concatenate(
        [f1, f2, f1, f3, f2, f1, jnp.zeros((LANES - 48, z.coef), f32)], axis=0
    )
    freq_t[...] = table.T[:, :48].astype(bf16)
    before = before_table()

    loop(1, groups, lambda d: order_copy(d).wait())

    m = LANES // z.boxes
    lane8 = lax.broadcasted_iota(i32, (8, LANES), 1)
    for t in range(z.box_total // LANES):
        tile = jnp.broadcast_to(order_all[t * m], (8, LANES))
        for u in range(1, m):
            shifted = pltpu.roll(
                jnp.broadcast_to(order_all[t * m + u], (8, LANES)), u * z.boxes, 1
            )
            tile = jnp.where(lane8 >= u * z.boxes, shifted, tile)
        order_row[:, t * LANES : (t + 1) * LANES] = tile
    ids = order_row[0:1, :]
    at = lax.broadcasted_iota(i32, (1, z.box_total), 1)
    high_hot = sublane(z.digits, z.box_total) == (ids >> 5)
    owner_of = (at // z.boxes).astype(f32)
    label_of = lax.rem(at, z.boxes).astype(f32)
    finder = dot(
        jnp.concatenate(
            [jnp.where(high_hot, owner_of, 0.0), jnp.where(high_hot, label_of, 0.0)], axis=0
        ).astype(bf16),
        hot((ids & 31).astype(f32), 32),
        NT,
    ).astype(bf16)

    def find(box_ids):
        got = dot(finder, hot((box_ids & 31).astype(f32), 32))
        mine = sublane(z.digits, box_ids.shape[1]) == (box_ids >> 5)
        who = jnp.sum(jnp.where(mine, got[: z.digits], 0.0), axis=0, keepdims=True)
        label = jnp.sum(jnp.where(mine, got[z.digits :], 0.0), axis=0, keepdims=True)
        return who, label

    step_nodes = min(1024, z.nodes)
    for s in range(z.nodes // step_nodes):
        here = slice(s * step_nodes, (s + 1) * step_nodes)
        who, label = find(node_box[:, here])
        owner_row[:, here] = who
        fields[:, here] = two(
            jnp.concatenate(
                [pos[:, here], stg[:, here], label + 1.0, jnp.zeros_like(label)], axis=0
            )
        )

    hits = []
    for k in range(z.nodes // LANES):
        row = owner_row[:, k * LANES : (k + 1) * LANES]
        hits.append(jnp.where(sublane(groups, LANES).astype(f32) == row, 1.0, 0.0))
    rank, _ = ranks(hits, before, jnp.zeros((groups, LANES), f32))
    hot_src[...] = hot(jnp.concatenate(rank, axis=1), z.per_peer)

    near_ids = near_t[...]
    for v in range(z.near):
        row = near_ids[v : v + 1]
        _, label = find(row)
        near_vm[v : v + 1, : z.boxes] = jnp.where(row >= 0, label.astype(i32), z.boxes)
    near_copy = pltpu.make_async_copy(near_vm, near_sm, local_sem.at[1])
    near_copy.start()

    def node_copy(d):
        return pltpu.make_async_remote_copy(
            src_ref=pay.at[ahead(d)],
            dst_ref=recv.at[me],
            send_sem=node_sem.at[0, d - 1],
            recv_sem=node_sem.at[1, d - 1],
            device_id=place(ahead(d)),
            device_id_type=MESH,
        )

    per_step = min(8, groups)

    def make_payload(k):
        owners = owner_row[...].astype(bf16)
        f = fields[...]
        rows = []
        for u in range(per_step):
            g = ahead(1 + k * per_step + u)
            g16 = jnp.full((1, LANES), g, i32).astype(f32).astype(bf16)[:, :1]
            rows.append(jnp.where(owners == g16, f, jnp.zeros((), bf16)))
        made = dot(jnp.concatenate(rows, axis=0), hot_src[...], NT)
        for u in range(per_step):
            d = 1 + k * per_step + u
            pay[ahead(d)] = made[16 * u : 16 * u + 8] + made[16 * u + 8 : 16 * u + 16]

            @pl.when(d < groups)
            def _():
                node_copy(d).start()

    loop(0, groups // per_step, make_payload)
    recv[me] = pay[me]

    for j in range(z.boxes):
        from_box = jnp.where(source_t[:, j : j + 1] == ids, 1.0, 0.0).astype(bf16)
        of_kind = jnp.where(
            kind[j : j + 1, :] == sublane(z.kinds, z.entries), 1.0, 0.0
        ).astype(bf16)
        counts[z.kinds * j : z.kinds * (j + 1), :] = dot(of_kind, from_box).astype(bf16)

    def load_chunk(ref, c):
        parts_ = [ref[behind(c * z.per_chunk + v)] for v in range(z.per_chunk)]
        return parts_[0] if z.per_chunk == 1 else jnp.concatenate(parts_, axis=1)

    grouped[...] = jnp.zeros_like(grouped)

    def group_batch(t, carry):
        def arrive(d, c):
            @pl.when(d > 0)
            def _():
                node_copy(d).wait()

            return c

        first = t * z.batch * z.per_chunk
        lax.fori_loop(first, first + z.batch * z.per_chunk, arrive, 0)
        labels, hits, tables = [], [], []
        for u in range(z.batch):
            blk = load_chunk(recv, t * z.batch + u)
            label = blk[6:7]
            label_dst[t * z.batch + u] = label
            labels.append(label)
            tables.append(two(blk))
            for h in range(WIDE // LANES):
                part = label[:, h * LANES : (h + 1) * LANES]
                hits.append(
                    jnp.where((sublane(z.boxes, LANES) + 1).astype(f32) == part, 1.0, 0.0)
                )
        rank, carry = ranks(hits, before_table(), carry)
        per = WIDE // LANES
        for u in range(z.batch):
            row = jnp.concatenate(rank[u * per : (u + 1) * per], axis=1)
            row = jnp.where(labels[u] > 0.0, row, -1.0)
            cols = slice(u * WIDE, (u + 1) * WIDE)
            hot_dst[t, :, cols] = hot(row, z.per_box)
            label16 = labels[u].astype(bf16)
            for b in range(z.boxes):
                a_buf[16 * b : 16 * b + 16, cols] = jnp.where(
                    label16 == jnp.full((), b + 1, bf16), tables[u], jnp.zeros((), bf16)
                )
        grouped[...] += dot(a_buf[...], hot_dst[t], NT)
        return carry

    lax.fori_loop(0, z.chunks // z.batch, group_batch, jnp.zeros((z.boxes, LANES), f32))

    def box_waves(b):
        got = grouped[pl.ds(pl.multiple_of(16 * b, 16), 16), :]
        lan = got[0:8] + got[8:16]
        lanes[b] = lan
        p, s = lan[0:3], lan[3:6]
        n = z.per_box
        zero = jnp.zeros((1, n), f32)
        one = jnp.ones((1, n), f32)
        part = two(jnp.concatenate([s, zero, *cross_parts(s, p), zero], axis=0))
        parts[b] = part
        p1, p2 = got[0:3], got[8:11]
        square = p[0:1] * p[0:1] + p[1:2] * p[1:2] + p[2:3] * p[2:3]
        pad = jnp.zeros((14, n), f32)
        tgt_tab[b] = jnp.concatenate(
            [p1, p1, p2, p2, one, one, one, *pieces(square + core_square, 3), pad], axis=0
        ).astype(bf16)
        src = jnp.concatenate(
            [-2.0 * p1, -2.0 * p2, -2.0 * p1, -2.0 * p2, *pieces(square, 3), one, one, one,
             jnp.zeros((LANES - 18, n), f32)],
            axis=0,
        )
        src_tab[b] = src.T[:, :32].astype(bf16)
        o1, o2, o3 = pieces(
            jnp.concatenate(
                [p[0:1] - center[0, b], p[1:2] - center[1, b], p[2:3] - center[2, b], one,
                 jnp.zeros((4, n), f32)],
                axis=0,
            ),
            3,
        )
        stacked = jnp.concatenate([o3, o2, o2, o1, o1, o1], axis=0).astype(bf16)
        turns = dot(freq_t[...], stacked)
        rows = 32
        highs, lows = [], []
        for c in range(z.coef // rows):
            wave = cos_turns(turns[c * rows : (c + 1) * rows])
            high = wave.astype(bf16)
            highs.append(high)
            lows.append((wave - high.astype(f32)).astype(bf16))
        high = jnp.concatenate(highs, axis=0)
        low = jnp.concatenate(lows, axis=0)
        wave_hi[b] = high
        wave_lo[b] = low
        sums = dot(part, high, NT) + dot(part, low, NT)
        sums = sums[0:8] + sums[8:16]
        sums_f[pl.ds(b, 1), :] = (
            direction[0:1, :] * sums[0:1]
            + direction[1:2, :] * sums[1:2]
            + direction[2:3, :] * sums[2:3]
        )

    loop(0, z.boxes, box_waves)
    parts[z.boxes] = jnp.zeros_like(parts[z.boxes])
    lane32 = lax.broadcasted_iota(i32, (z.per_box, 32), 1)
    src_tab[z.boxes] = jnp.where((lane32 >= 15) & (lane32 < 18), 1.0, 0.0).astype(bf16)
    near_copy.wait()

    blocks[me_age, me_box] = sums_f[...].astype(bf16)

    def along_box(d):
        return pltpu.make_async_remote_copy(
            src_ref=blocks.at[me_age, me_box],
            dst_ref=blocks.at[me_age, me_box],
            send_sem=block_sem.at[0, d - 1],
            recv_sem=block_sem.at[1, d - 1],
            device_id={"age": me_age, "box": lax.rem(me_box + d, n_box)},
            device_id_type=MESH,
        )

    def along_age(d):
        return pltpu.make_async_remote_copy(
            src_ref=blocks.at[me_age],
            dst_ref=blocks.at[me_age],
            send_sem=block_sem.at[0, n_box - 2 + d],
            recv_sem=block_sem.at[1, n_box - 2 + d],
            device_id={"age": lax.rem(me_age + d, n_age), "box": me_box},
            device_id_type=MESH,
        )

    def near_box(b):
        sums = jnp.zeros((16, z.per_box), f32)
        target = tgt_tab[b]
        for v in range(z.near):
            j = jnp.clip(near_sm[v, b], 0, z.boxes)
            r = lax.rsqrt(dot(src_tab[j], target))
            sums = sums + dot(parts[j], (r * r * r).astype(bf16))
        sums = sums[0:8] + sums[8:16]
        at_b = lanes[b]
        pad = jnp.zeros((5, z.per_box), f32)
        near = jnp.concatenate([*cross_parts(sums[0:3], at_b[0:3]), pad], axis=0)
        near_vel[b] = (near - jnp.concatenate([sums[4:7], pad], axis=0)) * inv_four_pi

    first = z.boxes // 4
    loop(1, n_box, lambda d: along_box(d).start())
    loop(0, first, near_box)
    loop(1, n_box, lambda d: along_box(d).wait())
    loop(1, n_age, lambda d: along_age(d).start())
    loop(first, z.boxes, near_box)
    loop(1, n_age, lambda d: along_age(d).wait())
    load_translation.wait()

    every = dot(counts[...], blocks[...].reshape(z.box_total, z.coef))
    for h in range(z.coef // LANES):
        mixed[h] = every[:, h * LANES : (h + 1) * LANES]
    expansion = jnp.zeros((z.boxes, z.coef), f32)
    for t in range(z.kinds):
        rows = [mixed[h, pl.ds(t, z.boxes, stride=z.kinds), :] for h in range(z.coef // LANES)]
        expansion = expansion + dot(jnp.concatenate(rows, axis=1).astype(bf16), trans[t], NT)
    sums_f[...] = expansion

    def far_box(b):
        row = sums_f[pl.ds(b, 1), :]
        table = two(
            jnp.concatenate([direction[...] * row, jnp.zeros((5, z.coef), f32)], axis=0)
        )
        far = dot(table, wave_hi[b]) + dot(table, wave_lo[b])
        total = near_vel[b] + far[0:8] + far[8:16]
        v1, v2 = pieces(total[0:3], 2)
        vel[pl.ds(pl.multiple_of(8 * b, 8), 8), :] = jnp.concatenate(
            [v1, v2, jnp.zeros((2, z.per_box), f32)], axis=0
        )

    loop(0, z.boxes, far_box)

    def back_copy(d):
        return pltpu.make_async_remote_copy(
            src_ref=back.at[behind(d)],
            dst_ref=returned.at[me],
            send_sem=back_sem.at[0, d - 1],
            recv_sem=back_sem.at[1, d - 1],
            device_id=place(behind(d)),
            device_id_type=MESH,
        )

    def pick(made, row, kinds, start):
        total = jnp.zeros((8, row.shape[1]), f32)
        for k in range(kinds):
            total = total + jnp.where(row == float(k + start), made[8 * k : 8 * k + 8], 0.0)
        return total[0:3] + total[3:6]

    per_chunk = z.per_chunk

    def send_back(t):
        table = vel[...].astype(bf16)
        for u in range(z.batch):
            c = t * z.batch + u
            made = dot(table, hot_dst[t, :, u * WIDE : (u + 1) * WIDE])
            done = pick(made, label_dst[c], z.boxes, 1)
            for v in range(per_chunk):
                d = c * per_chunk + v
                back[behind(d)] = done[:, v * z.per_peer : (v + 1) * z.per_peer]

                @pl.when(d > 0)
                def _():
                    back_copy(d).start()

    loop(0, z.chunks // z.batch, send_back)
    returned[me] = back[me]
    loop(1, groups, lambda d: back_copy(d).wait())

    rows = []
    for g in range(groups):
        v1, v2 = pieces(returned[g], 2)
        rows.append(jnp.concatenate([v1, v2, jnp.zeros((2, z.per_peer), f32)], axis=0))
    table = jnp.concatenate(rows, axis=0).astype(bf16)
    for s in range(z.nodes // 512):
        here = slice(s * 512, (s + 1) * 512)
        made = dot(table, hot_src[:, here])
        out[:, here] = pick(made, owner_row[:, here], groups, 0)


def per_device(
    n_age,
    n_box,
    position,
    strength,
    node_box,
    box_order,
    box_center,
    near_list,
    m2l_source,
    m2l_type,
    basis_dir,
    basis_freq,
    basis_phase,
    translation,
):
    z = Sizes(
        n_age, n_box, position.shape[1], box_order.shape[0], basis_phase.shape[0],
        translation.shape[0], m2l_source.shape[1], near_list.shape[1],
    )
    vm = pl.BlockSpec(memory_space=pltpu.VMEM)
    sm = pl.BlockSpec(memory_space=pltpu.SMEM)
    dma = pltpu.SemaphoreType.DMA

    def buf(shape, dtype=f32):
        return pltpu.VMEM(shape, dtype)

    return pl.pallas_call(
        functools.partial(body, z),
        out_shape=jax.ShapeDtypeStruct((3, z.nodes), f32),
        in_specs=[vm, vm, vm, vm, sm, vm, vm, vm, vm, vm, vm, pl.BlockSpec(memory_space=pl.ANY)],
        out_specs=vm,
        scratch_shapes=[
            buf((1, LANES), i32),
            buf((z.groups, 1, LANES), i32),
            buf((8, z.box_total), i32),
            buf((z.groups, 8, z.per_peer)),
            buf((z.groups, 8, z.per_peer)),
            buf((n_age, n_box, z.boxes, z.coef), bf16),
            buf((z.groups, 3, z.per_peer)),
            buf((z.groups, 3, z.per_peer)),
            buf((8, LANES), i32),
            pltpu.SMEM((8, LANES), i32),
            buf(translation.shape, bf16),
            buf((16, z.nodes), bf16),
            buf((z.per_peer, z.nodes), bf16),
            buf((1, z.nodes)),
            buf((16 * z.boxes, z.batch * WIDE), bf16),
            buf((z.chunks // z.batch, z.per_box, z.batch * WIDE), bf16),
            buf((z.chunks, 1, WIDE)),
            buf((16 * z.boxes, z.per_box)),
            buf((z.boxes, 8, z.per_box)),
            buf((z.boxes + 1, 16, z.per_box), bf16),
            buf((z.boxes + 1, z.per_box, 32), bf16),
            buf((z.boxes, 32, z.per_box), bf16),
            buf((z.coef, 48), bf16),
            buf((z.boxes, z.coef, z.per_box), bf16),
            buf((z.boxes, z.coef, z.per_box), bf16),
            buf((z.boxes, z.coef)),
            buf((z.kinds * z.boxes, z.box_total), bf16),
            buf((z.coef // LANES, z.kinds * z.boxes, LANES)),
            buf((z.boxes, 8, z.per_box)),
            buf((8 * z.boxes, z.per_box)),
            dma((2,)),
            dma((2, z.groups - 1)),
            dma((2, z.groups - 1)),
            dma((2, n_age + n_box - 2)),
            dma((2, z.groups - 1)),
        ],
        compiler_params=pltpu.CompilerParams(
            collective_id=0, has_side_effects=True, vmem_limit_bytes=VMEM_LIMIT
        ),
    )(
        position,
        strength,
        node_box.reshape(1, -1),
        box_order.reshape(1, -1),
        box_center,
        near_list.T,
        m2l_source.T,
        m2l_type,
        basis_dir,
        basis_freq,
        basis_phase.reshape(1, -1),
        translation,
    )


def solution(mesh):
    n_box = mesh.shape["box"]
    n_age = mesh.shape["age"]
    placed = (
        P(None, AXES),
        P(None, AXES),
        P(AXES),
        P(AXES),
        P(None, AXES),
        P(AXES, None),
        P(AXES, None),
        P(AXES, None),
        P(),
        P(),
        P(),
        P(),
    )
    return jax.shard_map(
        functools.partial(per_device, n_age, n_box),
        mesh=mesh,
        in_specs=placed,
        out_specs=P(None, AXES),
        check_vma=False,
    )
```

time: 143 us -> 78.5 us (0.55)
  Pallas kernels: 126 us -> 75.3 us
  other arithmetic: 6.5 us -> 0 us
  matrix products: 5.79 us -> 0 us
    pallas_call x9 -> x1, Pallas kernels: 126 us -> 75.3 us  [per_device(): pl.pallas_call(functools.partial(body, z), out_shape=jax.ShapeDtypeStruct...]
    dot_general x7 -> x0, matrix products: 5.79 us -> none  [the longest x2 2.14 us: ranks(): jnp.dot(hits16.reshape(kinds * blocks, LANES), before, preferred_element_...]
    reduce_sum x4 -> x0, other arithmetic: 4.51 us -> none  [the longest x1 3.03 us: per_device(): jnp.sum(jnp.where(node_box[None, :] == all_order[:, None], jnp.arange(box...]
    unnamed x10 -> x2, local copies, waits for them, and re-layouts: 0.02 us -> 2.88 us
where the time goes in v1:
time: 78.5 us; the launch traced here: 78.2 us
  Pallas kernels  75.3 us (96%)
  local copies, waits for them, and re-layouts  2.88 us (4%)
    pallas_call x1, Pallas kernels, per_device(): pl.pallas_call(functools.partial(body, z), out_shape=jax.ShapeDtypeStruct...  75.3 us
    unnamed x2, local copies, waits for them, and re-layouts  2.88 us

profile of v1, /device:TPU:0, one launch (start us, length us, event | category | flops | bytes accessed | tf_op | source)
XLA Modules:
  0.0 78.2 jit_solution(41673715170111551)
XLA Ops:
  0.0 1.4 %copy.13 = s32[32,32]{0,1:T(8,128)} copy(s32[32,32]{1,0:T(8,128)} %param.18) | data formatting | bytes 8192 | tf_op args[6]
  1.4 75.3 %shard_map.118 = f32[3,4096]{1,0:T(4,128)} custom-call(f32[3,4096]{1,0:T(4,128)} %pos.1, f32[3,4096]{1,0:T(4,128)} %stg.1, s32[1,4096]{1,0:T(1,128)} %bitcast.6, s32[1,32]{1,0:T(1,128)} %bitcast.9, f32[3,32]{1,0:T(4,128)} %center.1, s32[4,32]{1,0:T(4,128)} %bitcast.7, s32[32,32]{1,0:T(8,128)} %bitcast.5, s32[32,32]{1,0:T(8,128)} %kind.1, ...), custom_call_target="tpu_custom_call" | custom-call | tf_op jit(solution)/shard_map/pallas_call | solution.py:516
  76.7 1.5 %copy.15 = f32[3,4096]{1,0:T(4,128)} copy(f32[3,4096]{1,0:T(4,128)} %shard_map.118) | data formatting | bytes 98304

commit v2 on v1

--- a/solution.py
+++ b/solution.py
@@ -30,7 +30,7 @@
     return [float(c) for c in fit.convert(kind=np.polynomial.Polynomial).coef]
 
 
-COS_COEF = cos_coefficients(6)
+COS_COEF = cos_coefficients(5)
 
 
 def cos_turns(turns):
@@ -110,7 +110,7 @@
 
 def body(
     z,
-    pos, stg, node_box, order, center, near_t, source_t, kind, direction, freq, phase, translation,
+    pos, stg, node_box, order, center, near_t, source, kind, direction, freq, phase, translation,
     out,
     order_own, order_all, order_row, pay, recv, blocks, back, returned,
     near_vm, near_sm, trans, fields, hot_src, owner_row, a_buf, hot_dst, label_dst,
@@ -131,12 +131,12 @@
     def behind(d):
         return lax.rem(me + groups - d, groups)
 
-    def loop(lo, hi, f):
+    def loop(lo, hi, f, unroll=1):
         def step(i, carry):
             f(i)
             return carry
 
-        lax.fori_loop(lo, hi, step, 0)
+        lax.fori_loop(lo, hi, step, 0, unroll=unroll)
 
     loop(
         1, groups,
@@ -255,14 +255,17 @@
         for u in range(per_step):
             d = 1 + k * per_step + u
             pay[ahead(d)] = made[16 * u : 16 * u + 8] + made[16 * u + 8 : 16 * u + 16]
-
-            @pl.when(d < groups)
-            def _():
-                node_copy(d).start()
+        start = 1 + k * per_step
+        loop(start, jnp.minimum(start + per_step, groups), lambda d: node_copy(d).start())
 
     loop(0, groups // per_step, make_payload)
     recv[me] = pay[me]
 
+    square = jnp.concatenate(
+        [source[...], jnp.zeros((z.boxes, LANES - z.entries), i32)], axis=1
+    ).astype(f32)
+    square = jnp.concatenate([square, jnp.zeros((LANES - z.boxes, LANES), f32)], axis=0)
+    source_t = square.T[: z.entries].astype(i32)
     for j in range(z.boxes):
         from_box = jnp.where(source_t[:, j : j + 1] == ids, 1.0, 0.0).astype(bf16)
         of_kind = jnp.where(
@@ -366,7 +369,7 @@
             + direction[2:3, :] * sums[2:3]
         )
 
-    loop(0, z.boxes, box_waves)
+    loop(0, z.boxes, box_waves, 4)
     parts[z.boxes] = jnp.zeros_like(parts[z.boxes])
     lane32 = lax.broadcasted_iota(i32, (z.per_box, 32), 1)
     src_tab[z.boxes] = jnp.where((lane32 >= 15) & (lane32 < 18), 1.0, 0.0).astype(bf16)
@@ -397,10 +400,16 @@
     def near_box(b):
         sums = jnp.zeros((16, z.per_box), f32)
         target = tgt_tab[b]
-        for v in range(z.near):
-            j = jnp.clip(near_sm[v, b], 0, z.boxes)
-            r = lax.rsqrt(dot(src_tab[j], target))
-            sums = sums + dot(parts[j], (r * r * r).astype(bf16))
+        for first_v in range(0, z.near, 2):
+            picks = [
+                jnp.clip(near_sm[v, b], 0, z.boxes) for v in range(first_v, min(first_v + 2, z.near))
+            ]
+            factors = []
+            for j in picks:
+                r = lax.rsqrt(dot(src_tab[j], target))
+                factors.append((r * r * r).astype(bf16))
+            for j, factor in zip(picks, factors):
+                sums = sums + dot(parts[j], factor)
         sums = sums[0:8] + sums[8:16]
         at_b = lanes[b]
         pad = jnp.zeros((5, z.per_box), f32)
@@ -409,10 +418,10 @@
 
     first = z.boxes // 4
     loop(1, n_box, lambda d: along_box(d).start())
-    loop(0, first, near_box)
+    loop(0, first, near_box, 2)
     loop(1, n_box, lambda d: along_box(d).wait())
     loop(1, n_age, lambda d: along_age(d).start())
-    loop(first, z.boxes, near_box)
+    loop(first, z.boxes, near_box, 2)
     loop(1, n_age, lambda d: along_age(d).wait())
     load_translation.wait()
 
@@ -437,7 +446,7 @@
             [v1, v2, jnp.zeros((2, z.per_box), f32)], axis=0
         )
 
-    loop(0, z.boxes, far_box)
+    loop(0, z.boxes, far_box, 8)
 
     def back_copy(d):
         return pltpu.make_async_remote_copy(
@@ -466,10 +475,10 @@
             for v in range(per_chunk):
                 d = c * per_chunk + v
                 back[behind(d)] = done[:, v * z.per_peer : (v + 1) * z.per_peer]
-
-                @pl.when(d > 0)
-                def _():
-                    back_copy(d).start()
+        start = t * z.batch * per_chunk
+        loop(
+            jnp.maximum(start, 1), start + z.batch * per_chunk, lambda d: back_copy(d).start()
+        )
 
     loop(0, z.chunks // z.batch, send_back)
     returned[me] = back[me]
@@ -565,7 +574,7 @@
         box_order.reshape(1, -1),
         box_center,
         near_list.T,
-        m2l_source.T,
+        m2l_source,
         m2l_type,
         basis_dir,
         basis_freq,

time: 78.5 us -> 64.9 us (0.83)
  Pallas kernels: 75.3 us -> 63.2 us
  local copies, waits for them, and re-layouts: 2.88 us -> 1.48 us
    pallas_call x1, Pallas kernels: 75.3 us -> 63.2 us  [per_device(): pl.pallas_call(functools.partial(body, z), out_shape=jax.ShapeDtypeStruct...]
    unnamed x2 -> x1, local copies, waits for them, and re-layouts: 2.88 us -> 1.48 us
where the time goes in v2:
time: 64.9 us; the launch traced here: 64.6 us
  Pallas kernels  63.2 us (97%)
  local copies, waits for them, and re-layouts  1.48 us (2%)
    pallas_call x1, Pallas kernels, per_device(): pl.pallas_call(functools.partial(body, z), out_shape=jax.ShapeDtypeStruct...  63.2 us
    unnamed x1, local copies, waits for them, and re-layouts  1.48 us

profile of v2, /device:TPU:0, one launch (start us, length us, event | category | flops | bytes accessed | tf_op | source)
XLA Modules:
  0.0 64.6 jit_solution(14722181838791979863)
XLA Ops:
  0.0 63.2 %shard_map.118 = f32[3,4096]{1,0:T(4,128)} custom-call(f32[3,4096]{1,0:T(4,128)} %pos.1, f32[3,4096]{1,0:T(4,128)} %stg.1, s32[1,4096]{1,0:T(1,128)} %bitcast.4, s32[1,32]{1,0:T(1,128)} %bitcast.7, f32[3,32]{1,0:T(4,128)} %center.1, s32[4,32]{1,0:T(4,128)} %bitcast.5, s32[32,32]{1,0:T(8,128)} %source.1, s32[32,32]{1,0:T(8,128)} %kind.1, f32[3,256]{1,0:T(4,128)} %direction.1, ...), custom_call_target="tpu_custom_call" | custom-call | tf_op jit(solution)/shard_map/pallas_call | solution.py:525
  63.2 1.5 %copy.14 = f32[3,4096]{1,0:T(4,128)} copy(f32[3,4096]{1,0:T(4,128)} %shard_map.118) | data formatting | bytes 98304

commit v3 on v2

--- a/solution.py
+++ b/solution.py
@@ -233,8 +233,8 @@
 
     def node_copy(d):
         return pltpu.make_async_remote_copy(
-            src_ref=pay.at[ahead(d)],
-            dst_ref=recv.at[me],
+            src_ref=pay.at[ahead(d), pl.ds(0, 7)],
+            dst_ref=recv.at[me, pl.ds(0, 7)],
             send_sem=node_sem.at[0, d - 1],
             recv_sem=node_sem.at[1, d - 1],
             device_id=place(ahead(d)),
@@ -295,7 +295,7 @@
             label = blk[6:7]
             label_dst[t * z.batch + u] = label
             labels.append(label)
-            tables.append(two(blk))
+            tables.append(two(jnp.where(sublane(8, WIDE) < 7, blk, 0.0)))
             for h in range(WIDE // LANES):
                 part = label[:, h * LANES : (h + 1) * LANES]
                 hits.append(
@@ -400,16 +400,17 @@
     def near_box(b):
         sums = jnp.zeros((16, z.per_box), f32)
         target = tgt_tab[b]
-        for first_v in range(0, z.near, 2):
-            picks = [
-                jnp.clip(near_sm[v, b], 0, z.boxes) for v in range(first_v, min(first_v + 2, z.near))
-            ]
+        picks = [jnp.clip(near_sm[v, b], 0, z.boxes) for v in range(z.near)]
+        for at in range(0, z.near, 4):
+            some = picks[at : at + 4]
             factors = []
-            for j in picks:
+            for j in some:
                 r = lax.rsqrt(dot(src_tab[j], target))
                 factors.append((r * r * r).astype(bf16))
-            for j, factor in zip(picks, factors):
-                sums = sums + dot(parts[j], factor)
+            sums = sums + dot(
+                jnp.concatenate([parts[j] for j in some], axis=1),
+                jnp.concatenate(factors, axis=0),
+            )
         sums = sums[0:8] + sums[8:16]
         at_b = lanes[b]
         pad = jnp.zeros((5, z.per_box), f32)
@@ -418,10 +419,10 @@
 
     first = z.boxes // 4
     loop(1, n_box, lambda d: along_box(d).start())
-    loop(0, first, near_box, 2)
+    loop(0, first, near_box, 4)
     loop(1, n_box, lambda d: along_box(d).wait())
     loop(1, n_age, lambda d: along_age(d).start())
-    loop(first, z.boxes, near_box, 2)
+    loop(first, z.boxes, near_box, 4)
     loop(1, n_age, lambda d: along_age(d).wait())
     load_translation.wait()
 
@@ -459,9 +460,10 @@
         )
 
     def pick(made, row, kinds, start):
-        total = jnp.zeros((8, row.shape[1]), f32)
-        for k in range(kinds):
-            total = total + jnp.where(row == float(k + start), made[8 * k : 8 * k + 8], 0.0)
+        total = made[0:8]
+        for k in range(1, kinds):
+            total = jnp.where(row == float(k + start), made[8 * k : 8 * k + 8], total)
+        total = jnp.where(row >= float(start), total, 0.0)
         return total[0:3] + total[3:6]
 
     per_chunk = z.per_chunk

time: 64.9 us -> 59.7 us (0.920)
  Pallas kernels: 63.2 us -> 58 us
    pallas_call x1, Pallas kernels: 63.2 us -> 58 us  [per_device(): pl.pallas_call(functools.partial(body, z), out_shape=jax.ShapeDtypeStruct...]
where the time goes in v3:
time: 59.7 us; the launch traced here: 59.5 us
  Pallas kernels  58 us (97%)
  local copies, waits for them, and re-layouts  1.48 us (2%)
    pallas_call x1, Pallas kernels, per_device(): pl.pallas_call(functools.partial(body, z), out_shape=jax.ShapeDtypeStruct...  58 us
    unnamed x1, local copies, waits for them, and re-layouts  1.48 us

profile of v3, /device:TPU:0, one launch (start us, length us, event | category | flops | bytes accessed | tf_op | source)
XLA Modules:
  0.0 59.5 jit_solution(1851656921443403563)
XLA Ops:
  0.0 58.0 %shard_map.118 = f32[3,4096]{1,0:T(4,128)} custom-call(f32[3,4096]{1,0:T(4,128)} %pos.1, f32[3,4096]{1,0:T(4,128)} %stg.1, s32[1,4096]{1,0:T(1,128)} %bitcast.4, s32[1,32]{1,0:T(1,128)} %bitcast.7, f32[3,32]{1,0:T(4,128)} %center.1, s32[4,32]{1,0:T(4,128)} %bitcast.5, s32[32,32]{1,0:T(8,128)} %source.1, s32[32,32]{1,0:T(8,128)} %kind.1, f32[3,256]{1,0:T(4,128)} %direction.1, ...), custom_call_target="tpu_custom_call" | custom-call | tf_op jit(solution)/shard_map/pallas_call | solution.py:527
  58.0 1.5 %copy.14 = f32[3,4096]{1,0:T(4,128)} copy(f32[3,4096]{1,0:T(4,128)} %shard_map.118) | data formatting | bytes 98304

commit v4 on v3

--- a/solution.py
+++ b/solution.py
@@ -417,7 +417,7 @@
         near = jnp.concatenate([*cross_parts(sums[0:3], at_b[0:3]), pad], axis=0)
         near_vel[b] = (near - jnp.concatenate([sums[4:7], pad], axis=0)) * inv_four_pi
 
-    first = z.boxes // 4
+    first = 3 * z.boxes // 8
     loop(1, n_box, lambda d: along_box(d).start())
     loop(0, first, near_box, 4)
     loop(1, n_box, lambda d: along_box(d).wait())
@@ -442,12 +442,9 @@
         )
         far = dot(table, wave_hi[b]) + dot(table, wave_lo[b])
         total = near_vel[b] + far[0:8] + far[8:16]
-        v1, v2 = pieces(total[0:3], 2)
-        vel[pl.ds(pl.multiple_of(8 * b, 8), 8), :] = jnp.concatenate(
-            [v1, v2, jnp.zeros((2, z.per_box), f32)], axis=0
-        )
-
-    loop(0, z.boxes, far_box, 8)
+        vel[b] = total[0:4]
+
+    loop(0, z.boxes, far_box, 16)
 
     def back_copy(d):
         return pltpu.make_async_remote_copy(
@@ -459,20 +456,28 @@
             device_id_type=MESH,
         )
 
+    def spread(ref, rows):
+        high, low = pieces(ref[...].reshape(rows, ref.shape[2]), 2)
+        return high.astype(bf16), low.astype(bf16)
+
     def pick(made, row, kinds, start):
+        half = sublane(8, row.shape[1]) // 4
+        even = jnp.where(half == 0, row, row - 1.0)
         total = made[0:8]
-        for k in range(1, kinds):
-            total = jnp.where(row == float(k + start), made[8 * k : 8 * k + 8], total)
+        for k in range(2, kinds, 2):
+            total = jnp.where(even == float(k + start), made[4 * k : 4 * k + 8], total)
+        total = jnp.where(lax.rem((row - start).astype(i32), 2) == half, total, 0.0)
         total = jnp.where(row >= float(start), total, 0.0)
-        return total[0:3] + total[3:6]
+        return total[0:4] + total[4:8]
 
     per_chunk = z.per_chunk
 
     def send_back(t):
-        table = vel[...].astype(bf16)
+        high, low = spread(vel, 4 * z.boxes)
         for u in range(z.batch):
             c = t * z.batch + u
-            made = dot(table, hot_dst[t, :, u * WIDE : (u + 1) * WIDE])
+            hot_u = hot_dst[t, :, u * WIDE : (u + 1) * WIDE]
+            made = dot(high, hot_u) + dot(low, hot_u)
             done = pick(made, label_dst[c], z.boxes, 1)
             for v in range(per_chunk):
                 d = c * per_chunk + v
@@ -486,15 +491,11 @@
     returned[me] = back[me]
     loop(1, groups, lambda d: back_copy(d).wait())
 
-    rows = []
-    for g in range(groups):
-        v1, v2 = pieces(returned[g], 2)
-        rows.append(jnp.concatenate([v1, v2, jnp.zeros((2, z.per_peer), f32)], axis=0))
-    table = jnp.concatenate(rows, axis=0).astype(bf16)
+    high, low = spread(returned, 4 * groups)
     for s in range(z.nodes // 512):
         here = slice(s * 512, (s + 1) * 512)
-        made = dot(table, hot_src[:, here])
-        out[:, here] = pick(made, owner_row[:, here], groups, 0)
+        made = dot(high, hot_src[:, here]) + dot(low, hot_src[:, here])
+        out[:, here] = pick(made, owner_row[:, here], groups, 0)[0:3]
 
 
 def per_device(
@@ -536,8 +537,8 @@
             buf((z.groups, 8, z.per_peer)),
             buf((z.groups, 8, z.per_peer)),
             buf((n_age, n_box, z.boxes, z.coef), bf16),
-            buf((z.groups, 3, z.per_peer)),
-            buf((z.groups, 3, z.per_peer)),
+            buf((z.groups, 4, z.per_peer)),
+            buf((z.groups, 4, z.per_peer)),
             buf((8, LANES), i32),
             pltpu.SMEM((8, LANES), i32),
             buf(translation.shape, bf16),
@@ -559,7 +560,7 @@
             buf((z.kinds * z.boxes, z.box_total), bf16),
             buf((z.coef // LANES, z.kinds * z.boxes, LANES)),
             buf((z.boxes, 8, z.per_box)),
-            buf((8 * z.boxes, z.per_box)),
+            buf((z.boxes, 4, z.per_box)),
             dma((2,)),
             dma((2, z.groups - 1)),
             dma((2, z.groups - 1)),

time: 59.7 us -> 58.8 us (0.985)
  Pallas kernels: 58 us -> 57.1 us
    pallas_call x1, Pallas kernels: 58 us -> 57.1 us  [per_device(): pl.pallas_call(functools.partial(body, z), out_shape=jax.ShapeDtypeStruct...]
where the time goes in v4:
time: 58.8 us; the launch traced here: 58.6 us
  Pallas kernels  57.1 us (97%)
  local copies, waits for them, and re-layouts  1.48 us (3%)
    pallas_call x1, Pallas kernels, per_device(): pl.pallas_call(functools.partial(body, z), out_shape=jax.ShapeDtypeStruct...  57.1 us
    unnamed x1, local copies, waits for them, and re-layouts  1.48 us

profile of v4, /device:TPU:0, one launch (start us, length us, event | category | flops | bytes accessed | tf_op | source)
XLA Modules:
  0.0 58.6 jit_solution(9704434036840528735)
XLA Ops:
  0.0 57.1 %shard_map.118 = f32[3,4096]{1,0:T(4,128)} custom-call(f32[3,4096]{1,0:T(4,128)} %pos.1, f32[3,4096]{1,0:T(4,128)} %stg.1, s32[1,4096]{1,0:T(1,128)} %bitcast.4, s32[1,32]{1,0:T(1,128)} %bitcast.7, f32[3,32]{1,0:T(4,128)} %center.1, s32[4,32]{1,0:T(4,128)} %bitcast.5, s32[32,32]{1,0:T(8,128)} %source.1, s32[32,32]{1,0:T(8,128)} %kind.1, f32[3,256]{1,0:T(4,128)} %direction.1, ...), custom_call_target="tpu_custom_call" | custom-call | tf_op jit(solution)/shard_map/pallas_call | solution.py:528
  57.1 1.5 %copy.14 = f32[3,4096]{1,0:T(4,128)} copy(f32[3,4096]{1,0:T(4,128)} %shard_map.118) | data formatting | bytes 98304

commit v5 on v4

--- a/solution.py
+++ b/solution.py
@@ -31,14 +31,15 @@
 
 
 COS_COEF = cos_coefficients(5)
+COS_TOP = COS_COEF[-1]
 
 
 def cos_turns(turns):
     v = turns - ((turns + 12582912.0) - 12582912.0)
     w = v * v
-    acc = jnp.full_like(w, COS_COEF[-1])
-    for c in COS_COEF[-2::-1]:
-        acc = acc * w + c
+    acc = w + COS_COEF[-2] / COS_TOP
+    for c in COS_COEF[-3::-1]:
+        acc = acc * w + c / COS_TOP
     return acc
 
 
@@ -363,7 +364,7 @@
         wave_lo[b] = low
         sums = dot(part, high, NT) + dot(part, low, NT)
         sums = sums[0:8] + sums[8:16]
-        sums_f[pl.ds(b, 1), :] = (
+        sums_f[pl.ds(b, 1), :] = COS_TOP * (
             direction[0:1, :] * sums[0:1]
             + direction[1:2, :] * sums[1:2]
             + direction[2:3, :] * sums[2:3]
@@ -436,7 +437,7 @@
     sums_f[...] = expansion
 
     def far_box(b):
-        row = sums_f[pl.ds(b, 1), :]
+        row = sums_f[pl.ds(b, 1), :] * COS_TOP
         table = two(
             jnp.concatenate([direction[...] * row, jnp.zeros((5, z.coef), f32)], axis=0)
         )

time: 58.8 us -> 58.6 us (level)
  no operation moved by 1% of the time
where the time goes in v5:
time: 58.6 us; the launch traced here: 58.4 us
  Pallas kernels  56.9 us (97%)
  local copies, waits for them, and re-layouts  1.48 us (3%)
    pallas_call x1, Pallas kernels, per_device(): pl.pallas_call(functools.partial(body, z), out_shape=jax.ShapeDtypeStruct...  56.9 us
    unnamed x1, local copies, waits for them, and re-layouts  1.48 us

profile of v5, /device:TPU:0, one launch (start us, length us, event | category | flops | bytes accessed | tf_op | source)
XLA Modules:
  0.0 58.4 jit_solution(17267900903139573919)
XLA Ops:
  0.0 56.9 %shard_map.118 = f32[3,4096]{1,0:T(4,128)} custom-call(f32[3,4096]{1,0:T(4,128)} %pos.1, f32[3,4096]{1,0:T(4,128)} %stg.1, s32[1,4096]{1,0:T(1,128)} %bitcast.4, s32[1,32]{1,0:T(1,128)} %bitcast.7, f32[3,32]{1,0:T(4,128)} %center.1, s32[4,32]{1,0:T(4,128)} %bitcast.5, s32[32,32]{1,0:T(8,128)} %source.1, s32[32,32]{1,0:T(8,128)} %kind.1, f32[3,256]{1,0:T(4,128)} %direction.1, ...), custom_call_target="tpu_custom_call" | custom-call | tf_op jit(solution)/shard_map/pallas_call | solution.py:529
  56.9 1.5 %copy.14 = f32[3,4096]{1,0:T(4,128)} copy(f32[3,4096]{1,0:T(4,128)} %shard_map.118) | data formatting | bytes 98304
